TPU v7x, 512 devices: a whole 4x8x8 slice. The times are simulated.
512 devices in a mesh: island: 16 (over z, x_lo), shard: 32 (over y, x_hi, core).
Axes of the slice: x: 4 (x_hi: 2, x_lo: 2; x = x_hi * 2 + x_lo), y: 8, z: 8, core: 2. Of those that a mesh axis runs over, the one named last changes fastest.
Arguments:
- island_params: float32 [16, 2, 256, 4096], P('island', None, 'shard'), may hold values from -6 to 6
- outer_params: float32 [16, 1, 256, 4096], P('island', None, 'shard'), may hold values from -6 to 6
- momentum: float32 [16, 1, 256, 4096], P('island', None, 'shard'), may hold values from -3 to 3
- path_modules: int32 [16, 2], replicated, may hold values from 0 to 15, as said below
- owner_modules: int32 [16, 1], replicated, may hold values from 0 to 15, as said below
Outputs:
- new_params: float32 [16, 2, 256, 4096], P('island', None, 'shard')
- new_outer: float32 [16, 1, 256, 4096], P('island', None, 'shard')
- new_momentum: float32 [16, 1, 256, 4096], P('island', None, 'shard')
Inputs may be any that keep to these rules, and one draw needn't show every extreme that they name: `path_modules`: column 0 names the level-one module (below 8) of island i's path and column 1 its level-two module (from 8 on); in each level some module is named by no island. `owner_modules`: every module stands in exactly one slot of one island.
All inputs are finite; a program needn't handle non-finite values.
Results may differ from a plain program's by a relative error of at most 0.00002.
Values sent between devices are 32-bit elements; how exact they have to be, the bound alone decides.
A program may use at most 64 MiB of HBM per device.

v0:
```python
import jax
import jax.numpy as jnp
from jax import lax
from jax.sharding import PartitionSpec as P

momentum_rate = 0.9
outer_rate = 0.7


def body(island_params, outer_params, momentum, path_modules, owner_modules):
    position = lax.axis_index("island")
    per_owner = owner_modules.shape[1]
    modules = owner_modules.shape[0] * per_owner
    module_ids = jnp.arange(modules, dtype=jnp.int32)
    usage_hits = (path_modules[:, :, None] == module_ids[None, None, :]).astype(jnp.float32)
    sharers = jnp.sum(usage_hits, axis=(0, 1))
    my_path = lax.dynamic_slice_in_dim(path_modules, position, 1, 0)[0]
    my_owned = lax.dynamic_slice_in_dim(owner_modules, position, 1, 0)[0]
    owned_hit = my_owned[:, None] == module_ids[None, :]
    owned_sharers = jnp.sum(jnp.where(owned_hit, sharers[None, :], 0.0), axis=1)
    local_params = island_params[0]
    outer_held = outer_params[0]
    moment_held = momentum[0]
    placed = jnp.where(
        (module_ids == my_path[0])[:, None, None],
        local_params[0][None],
        jnp.where((module_ids == my_path[1])[:, None, None], local_params[1][None], 0.0),
    )
    summed_all = lax.psum(placed, "island")
    weight = owned_sharers[:, None, None]
    pseudo_grad = (weight * outer_held - summed_all[my_owned]) / jnp.maximum(weight, 1.0)
    moment = momentum_rate * moment_held + pseudo_grad
    updated = outer_held - outer_rate * (pseudo_grad + momentum_rate * moment)
    updated, moment = (updated, moment)
    spread = jnp.zeros((modules,) + updated.shape[1:], jnp.float32).at[my_owned].set(updated)
    returned = lax.psum(spread, "island")
    new_params = returned[my_path]
    return (new_params[None], updated[None], moment[None])


def solution(mesh):
    placed = (
        P("island", None, "shard", None),
        P("island", None, "shard", None),
        P("island", None, "shard", None),
        P(),
        P(),
    )
    return jax.shard_map(
        body,
        mesh=mesh,
        in_specs=placed,
        out_specs=(
            P("island", None, "shard", None),
            P("island", None, "shard", None),
            P("island", None, "shard", None),
        ),
        check_vma=False,
    )
```

profile of v0, /device:TPU:56, one launch (start us, length us, event | category | flops | bytes accessed | tf_op | source)
XLA Modules:
  0.0 333.4 jit_solution(16971092508905933627)
XLA Ops:
  7.2 0.0 copy-start
  7.2 0.0 all-reduce.3.cloned.1.call-start
  7.2 0.9 fusion.11
  8.1 0.5 fusion.12
  8.6 1.0 slice_bitcast_fusion.1
  9.6 1.3 iota_compare_fusion.1
  10.9 0.0 copy-start.4
  10.9 0.0 copy-start.5
  10.9 1.6 select_select_fusion
  12.6 0.0 copy-start.2
  12.6 0.0 copy-start.3
  12.6 0.0 all-reduce.3.cloned.1.call-update
  12.6 0.0 all-reduce.5.cloned.1.call-start
  12.7 0.0 copy-done
  12.7 0.6 constant_dynamic-slice_fusion.1
  15.2 0.0 copy-done.4
  15.2 0.1 convert_reduce_fusion
  15.3 1.2 fusion.9
  17.1 0.0 copy-done.5
  17.1 0.7 and_reduce_fusion
  17.8 151.5 %all-reduce.3.cloned.1.call-done = f32[16,8,4096]{2,1,0:T(8,128)} async-done(((f32[16,8,4096]{2,1,0:T(8,128)}), f32[16,8,4096]{2,1,0:T(8,128)}) %all-reduce.3.cloned.1.call-update) | async-done | bytes 2097168 | tf_op jit(solution)/shard_map/psum | solution.py:29
  169.3 0.2 broadcast_in_dim.62
  169.5 0.0 copy-done.2
  169.5 0.0 copy-done.3
  169.5 2.2 fusion.6
  171.7 0.0 copy-start.1
  171.7 1.3 copy-done.1
  173.0 0.0 all-reduce.5.cloned.1.call-update
  173.1 2.2 multiply_subtract_fusion
  175.3 148.4 %all-reduce.5.cloned.1.call-done = f32[16,8,4096]{2,1,0:T(8,128)} async-done(((f32[16,8,4096]{2,1,0:T(8,128)}), f32[16,8,4096]{2,1,0:T(8,128)}) %all-reduce.5.cloned.1.call-update) | async-done | bytes 2097168 | tf_op jit(solution)/shard_map/psum | solution.py:36
  323.8 2.9 gather_fusion
  (2 shorter events, 0.0 us)
Async XLA Ops:
  7.2 5.5 %copy-start = (s32[16,1]{0,1:T(1,128)S(1)}, s32[16,1]{0,1:T(1,128)}, u32[]{:S(2)}) copy-start(s32[16,1]{0,1:T(1,128)} %param.11) | copy-start | bytes 196
  7.2 162.1 %all-reduce.3.cloned.1.call-start = ((), (), s32[]{:S(2)}) async-start(), calls=%async_computation | async-start | bytes 4194304 | tf_op jit(solution)/shard_map/psum | solution.py:29
  10.9 4.3 %copy-start.4 = (s32[16,2]{0,1:T(2,128)S(1)}, s32[16,2]{0,1:T(2,128)}, u32[]{:S(2)}) copy-start(s32[16,2]{0,1:T(2,128)} %param.10) | copy-start | bytes 388
  10.9 6.2 %copy-start.5 = (s32[3]{0:T(128)S(1)}, s32[3]{0:T(128)}, u32[]{:S(2)}) copy-start(s32[3]{0:T(128)} %constant.42.clone.1) | copy-start | bytes 40
  12.6 156.9 %copy-start.2 = (f32[1,1,8,4096]{3,2,1,0:T(8,128)S(1)}, f32[1,1,8,4096]{3,2,1,0:T(8,128)}, u32[]{:S(2)}) copy-start(f32[1,1,8,4096]{3,2,1,0:T(8,128)} %param.8) | copy-start | bytes 393220
  12.6 156.9 %copy-start.3 = (f32[1,1,8,4096]{3,2,1,0:T(8,128)S(1)}, f32[1,1,8,4096]{3,2,1,0:T(8,128)}, u32[]{:S(2)}) copy-start(f32[1,1,8,4096]{3,2,1,0:T(8,128)} %param.9) | copy-start | bytes 393220
  12.6 311.2 %all-reduce.5.cloned.1.call-start = ((), (), s32[]{:S(2)}) async-start(), calls=%async_computation.1 | async-start | bytes 4194304 | tf_op jit(solution)/shard_map/psum | solution.py:36
  171.7 1.3 copy-start.1
Sparse Core Ops, SparseCore 0:
  12.7 156.5 all-reduce.2
  173.2 150.5 all-reduce.4
where the time goes:
time: 334 us; the launch traced here: 333 us
  waiting for transfers between devices  300 us (90%)
  between operations  16.7 us (5%)
  other arithmetic  9.41 us (3%)
  local copies, waits for them, and re-layouts  7.36 us (2%)
    psum x1, waiting for transfers between devices, body(): summed_all = lax.psum(placed, 'island')  151 us
    psum x1, waiting for transfers between devices, body(): returned = lax.psum(spread, 'island')  148 us
  transfers between devices with their start and end apart: 2, of which 2 were waited for; matrix products, arithmetic and copies ran while one was open for 1% of the time, Pallas kernels for 0%

commit v1 on v0

v1 whole, which is shorter than its diff:
```python
import functools

import jax
import jax.numpy as jnp
from jax import lax
from jax.experimental import pallas as pl
from jax.experimental.pallas import tpu as pltpu
from jax.sharding import PartitionSpec as P

momentum_rate = 0.9
outer_rate = 0.7
MESH = pl.DeviceIdType.MESH


def kernel(n, p_hbm, outer_hbm, mom_hbm, path, owner, par_out, outer_out, mom_out,
           p_v, outer_v, mom_v, base_v, arrived, table, stage, home, moment_v, weights, slot_of,
           load_sem, store_sem, send_p, recv_p, send_b, recv_b, send_u, recv_u):
    me = lax.axis_index("island")
    depth = p_v.shape[1]
    cols = p_v.shape[2] // n
    pairs = [(dz, dx) for dz in (4, 3, 5, 2, 6, 1, 7, 0) for dx in (1, 0)]
    offsets = [(dz % (n // 2), dx) for dz, dx in pairs if (dz % (n // 2), dx) != (0, 0)]
    z, x = me // 2, me % 2

    def ahead(k):
        dz, dx = offsets[k]
        return lax.rem(z + dz, n // 2) * 2 + lax.rem(x + dx, 2)

    def behind(k):
        dz, dx = offsets[k]
        return lax.rem(z + n // 2 - dz, n // 2) * 2 + lax.rem(x + dx, 2)

    peers = len(offsets)

    def span(j):
        return pl.ds(pl.multiple_of(j * cols, cols), cols)

    loads = [pltpu.make_async_copy(a, b, load_sem.at[i]) for i, (a, b) in enumerate(
        ((p_hbm.at[0], p_v), (outer_hbm.at[0, 0], outer_v), (mom_hbm.at[0, 0], mom_v)))]
    for c in loads:
        c.start()
    barrier = pltpu.get_barrier_semaphore()
    for k in range(peers):
        pl.semaphore_signal(barrier, inc=1, device_id={"island": ahead(k)}, device_id_type=MESH)
    pl.semaphore_wait(barrier, peers)
    loads[0].wait()

    def remote(src, dst, ssem, rsem, k):
        return pltpu.make_async_remote_copy(src_ref=src, dst_ref=dst, send_sem=ssem, recv_sem=rsem,
                                            device_id={"island": ahead(k)}, device_id_type=MESH)

    sends = []
    for k in range(peers):
        c = remote(p_v.at[:, :, span(ahead(k))], arrived.at[k, 0:2], send_p.at[k], recv_p.at[k], k)
        c.start()
        sends.append(c)
    loads[1].wait()
    loads[2].wait()
    mine = owner[me, 0]
    used = jnp.int32(0)
    for j in range(n):
        for l in range(2):
            used += (path[j, l] == mine).astype(jnp.int32)
    hit = jnp.minimum(used, 1).astype(jnp.float32)
    keep = 1.0 - outer_rate * (1.0 + momentum_rate) * hit
    base_v[...] = keep * outer_v[...] - (outer_rate * momentum_rate * momentum_rate) * mom_v[...]
    for k in range(peers):
        c = remote(base_v.at[:, span(ahead(k))], arrived.at[k, 2], send_b.at[k], recv_b.at[k], k)
        c.start()
        sends.append(c)
    arrived[peers, 0:2] = p_v[:, :, span(me)]
    arrived[peers, 2] = base_v[:, span(me)]

    sources = [behind(k) for k in range(peers)] + [me]
    for m in range(n):
        level = m // (n // 2)
        count = jnp.int32(0)
        holder = jnp.int32(0)
        for k in range(n):
            count += (path[sources[k], level] == m).astype(jnp.int32)
            holder = jnp.where(owner[sources[k], 0] == m, jnp.int32(k), holder)
        slot_of[m] = holder
        rate = outer_rate * (1.0 + momentum_rate) / jnp.maximum(
            jnp.full((1, 128), count.astype(jnp.float32)), 1.0)
        for k in range(n):
            f = (path[sources[k], level] == m).astype(jnp.float32)
            weights[pl.ds(m * n + k, 1), :] = rate * f

    for k in range(peers):
        remote(p_v.at[:, :, span(me)], arrived.at[k, 0:2], send_p.at[k], recv_p.at[k], k).wait_recv()
    for k in range(peers):
        remote(base_v.at[:, span(me)], arrived.at[k, 2], send_b.at[k], recv_b.at[k], k).wait_recv()

    half = n // 2
    for level in range(2):
        acc = [arrived[slot_of[level * half + m], 2] for m in range(half)]
        for k in range(n):
            v = arrived[k, level]
            for m in range(half):
                w = weights[pl.ds((level * half + m) * n + k, 1), :]
                w = jnp.concatenate([w] * (cols // 128), axis=1)
                acc[m] = acc[m] + w * v
        for m in range(half):
            table[level * half + m] = acc[m]

    for k in range(peers):
        to = ahead(k)
        stage[k, 0] = table[path[to, 0]]
        stage[k, 1] = table[path[to, 1]]
        stage[k, 2] = table[owner[to, 0]]
        c = remote(stage.at[k], home.at[:, :, span(me)], send_u.at[k], recv_u.at[k], k)
        c.start()
        sends.append(c)
    home[0, :, span(me)] = table[path[me, 0]]
    home[1, :, span(me)] = table[path[me, 1]]
    home[2, :, span(me)] = table[owner[me, 0]]
    for k in range(peers):
        remote(stage.at[k], home.at[:, :, span(behind(k))], send_u.at[k], recv_u.at[k], k).wait_recv()
    stores = [pltpu.make_async_copy(home.at[0:2], par_out.at[0], store_sem.at[0]),
              pltpu.make_async_copy(home.at[2], outer_out.at[0, 0], store_sem.at[1]),
              pltpu.make_async_copy(moment_v, mom_out.at[0, 0], store_sem.at[2])]
    stores[0].start()
    stores[1].start()
    moment_v[...] = ((outer_v[...] - home[2]) * (1.0 / outer_rate) + momentum_rate * mom_v[...]) * (
        1.0 / (1.0 + momentum_rate))
    stores[2].start()
    for c in sends:
        c.wait_send()
    for c in stores:
        c.wait()


def body(island_params, outer_params, momentum, path_modules, owner_modules):
    n = path_modules.shape[0]
    depth, width = island_params.shape[2:]
    cols = width // n
    f32 = jnp.float32
    any_ = pl.BlockSpec(memory_space=pl.ANY)
    smem = pl.BlockSpec(memory_space=pltpu.SMEM)
    return pl.pallas_call(
        functools.partial(kernel, n),
        out_shape=(jax.ShapeDtypeStruct(island_params.shape, f32),
                   jax.ShapeDtypeStruct(outer_params.shape, f32),
                   jax.ShapeDtypeStruct(momentum.shape, f32)),
        in_specs=[any_, any_, any_, smem, smem],
        out_specs=(any_, any_, any_),
        scratch_shapes=[
            pltpu.VMEM((2, depth, width), f32),
            pltpu.VMEM((depth, width), f32),
            pltpu.VMEM((depth, width), f32),
            pltpu.VMEM((depth, width), f32),
            pltpu.VMEM((n, 3, depth, cols), f32),
            pltpu.VMEM((n, depth, cols), f32),
            pltpu.VMEM((n, 3, depth, cols), f32),
            pltpu.VMEM((3, depth, width), f32),
            pltpu.VMEM((depth, width), f32),
            pltpu.VMEM((n * n, 128), f32),
            pltpu.SMEM((n,), jnp.int32),
            pltpu.SemaphoreType.DMA((3,)),
            pltpu.SemaphoreType.DMA((3,)),
        ] + [pltpu.SemaphoreType.DMA((n,))] * 6,
        compiler_params=pltpu.CompilerParams(collective_id=1, has_side_effects=True,
                                             vmem_limit_bytes=16 * 1024 * 1024),
        name="outer_step",
    )(island_params, outer_params, momentum, path_modules, owner_modules)


def solution(mesh):
    split = P("island", None, "shard", None)
    return jax.shard_map(
        body,
        mesh=mesh,
        in_specs=(split, split, split, P(), P()),
        out_specs=(split, split, split),
        check_vma=False,
    )
```

time: 334 us -> 41.8 us (0.13)
  waiting for transfers between devices: 300 us -> 0 us
  Pallas kernels: 0 us -> 35.3 us
  between operations: 16.7 us -> 0.65 us
  other arithmetic: 9.41 us -> 0 us
    psum x2 -> x0, waiting for transfers between devices: 300 us -> none  [the longest x1 151 us: body(): summed_all = lax.psum(placed, 'island')]
    pallas_call x0 -> x1, Pallas kernels: none -> 35.3 us  [body(): pl.pallas_call(functools.partial(kernel, n), out_shape=(jax.ShapeDtypeStr...]
    unnamed x12 -> x13, local copies, waits for them, and re-layouts: 1.35 us -> 5.62 us
  transfers between devices with their start and end apart: 2 -> 0, of which waited for: 2 -> 0; matrix products, arithmetic and copies ran while one was open for 1% -> 0% of each run, Pallas kernels for 0% -> 0%
where the time goes in v1:
time: 41.8 us; the launch traced here: 41.6 us
  Pallas kernels  35.3 us (84%)
  local copies, waits for them, and re-layouts  5.62 us (13%)
  between operations  0.65 us (2%)
    pallas_call x1, Pallas kernels, body(): pl.pallas_call(functools.partial(kernel, n), out_shape=(jax.ShapeDtypeStr...  35.3 us
    unnamed x13, local copies, waits for them, and re-layouts  5.62 us

profile of v1, /device:TPU:56, one launch (start us, length us, event | category | flops | bytes accessed | tf_op | source)
XLA Modules:
  0.0 41.6 jit_solution(12165190247619521521)
XLA Ops:
  0.6 0.0 copy-start.3
  0.6 0.8 %copy.8.path = s32[16,2]{1,0:T(8,128)S(1)} copy(s32[16,2]{0,1:T(2,128)} %param.8) | data formatting | bytes 256 | tf_op args[3]
  1.4 0.0 copy-done.3
  1.4 0.1 copy.9.owner
  1.5 0.0 copy-start
  1.5 0.9 %copy-done = f32[1,2,8,4096]{3,2,1,0:T(8,128)S(1)} copy-done((f32[1,2,8,4096]{3,2,1,0:T(8,128)S(1)}, f32[1,2,8,4096]{3,2,1,0:T(8,128)}, u32[]{:S(2)}) %copy-start) | copy-done | bytes 262168
  2.4 0.0 copy-start.1
  2.4 0.9 %copy-done.1 = f32[1,1,8,4096]{3,2,1,0:T(8,128)S(1)} copy-done((f32[1,1,8,4096]{3,2,1,0:T(8,128)S(1)}, f32[1,1,8,4096]{3,2,1,0:T(8,128)}, u32[]{:S(2)}) %copy-start.1) | copy-done | bytes 131096
  3.3 0.0 copy-start.2
  3.3 0.9 %copy-done.2 = f32[1,1,8,4096]{3,2,1,0:T(8,128)S(1)} copy-done((f32[1,1,8,4096]{3,2,1,0:T(8,128)S(1)}, f32[1,1,8,4096]{3,2,1,0:T(8,128)}, u32[]{:S(2)}) %copy-start.2) | copy-done | bytes 131096
  4.2 35.3 %outer_step.1 = (f32[1,2,8,4096]{3,2,1,0:T(8,128)S(1)}, f32[1,1,8,4096]{3,2,1,0:T(8,128)S(1)}, f32[1,1,8,4096]{3,2,1,0:T(8,128)S(1)}) custom-call(f32[1,2,8,4096]{3,2,1,0:T(8,128)S(1)} %copy-done, f32[1,1,8,4096]{3,2,1,0:T(8,128)S(1)} %copy-done.1, f32[1,1,8,4096]{3,2,1,0:T(8,128)S(1)} %copy-done.2, s32[16,2]{1,0:T(8,128)S(1)} %copy.8.path, ...), custom_call_target="tpu_custom_call" | custom-call | tf_op jit(solution)/shard_map/outer_step/pallas_call | solution.py:140
  39.5 0.7 %copy.13 = f32[1,2,8,4096]{3,2,1,0:T(8,128)} copy(f32[1,2,8,4096]{3,2,1,0:T(8,128)S(1)} %get-tuple-element.6) | data formatting | bytes 524288
  40.3 0.7 %copy.14 = f32[1,1,8,4096]{3,2,1,0:T(8,128)} copy(f32[1,1,8,4096]{3,2,1,0:T(8,128)S(1)} %get-tuple-element.7) | data formatting | bytes 262144
  40.9 0.7 %copy.15 = f32[1,1,8,4096]{3,2,1,0:T(8,128)} copy(f32[1,1,8,4096]{3,2,1,0:T(8,128)S(1)} %get-tuple-element.8) | data formatting | bytes 262144
Async XLA Ops:
  0.6 0.8 %copy-start.3 = (s32[16,1]{0,1:T(1,128)S(1)}, s32[16,1]{0,1:T(1,128)}, u32[]{:S(2)}) copy-start(s32[16,1]{0,1:T(1,128)} %param.9) | copy-start | bytes 196
  1.5 1.0 %copy-start = (f32[1,2,8,4096]{3,2,1,0:T(8,128)S(1)}, f32[1,2,8,4096]{3,2,1,0:T(8,128)}, u32[]{:S(2)}) copy-start(f32[1,2,8,4096]{3,2,1,0:T(8,128)} %p_hbm.1) | copy-start | bytes 786436
  2.4 0.9 %copy-start.1 = (f32[1,1,8,4096]{3,2,1,0:T(8,128)S(1)}, f32[1,1,8,4096]{3,2,1,0:T(8,128)}, u32[]{:S(2)}) copy-start(f32[1,1,8,4096]{3,2,1,0:T(8,128)} %outer_hbm.1) | copy-start | bytes 393220
  3.3 0.9 %copy-start.2 = (f32[1,1,8,4096]{3,2,1,0:T(8,128)S(1)}, f32[1,1,8,4096]{3,2,1,0:T(8,128)}, u32[]{:S(2)}) copy-start(f32[1,1,8,4096]{3,2,1,0:T(8,128)} %mom_hbm.1) | copy-start | bytes 393220

commit v2 on v0

v2 whole, which is shorter than its diff:
```python
import functools

import jax
import jax.numpy as jnp
from jax import lax
from jax.experimental import pallas as pl
from jax.experimental.pallas import tpu as pltpu
from jax.sharding import PartitionSpec as P

momentum_rate = 0.9
outer_rate = 0.7
both_rates = outer_rate * (1.0 + momentum_rate)
MESH = pl.DeviceIdType.MESH
ROOM = 60 * 1024 * 1024
chunks = 2


def relay(n, p_hbm, outer_hbm, mom_hbm, path_hbm, owner_hbm, home,
          path, owner, outer_v, mom_v, base_v, table, stage, weights, slot_of,
          load_sem, self_sem, send_p, recv_p, send_b, recv_b, send_u, recv_u, *arrived):
    me = lax.axis_index("island")
    ring = n // 2
    width = outer_v.shape[1]
    cols = width // n // chunks
    far_first = sorted(range(ring), key=lambda d: -min(d, ring - d))
    offsets = [(dz, dx) for dz in far_first for dx in (1, 0) if (dz, dx) != (0, 0)]
    peers = len(offsets)
    z, x = me // 2, me % 2

    def ahead(k):
        dz, dx = offsets[k]
        return lax.rem(z + dz, ring) * 2 + lax.rem(x + dx, 2)

    def behind(k):
        dz, dx = offsets[k]
        return lax.rem(z + ring - dz, ring) * 2 + lax.rem(x + dx, 2)

    def span(j, c):
        return pl.ds(pl.multiple_of(j * (cols * chunks) + c * cols, cols), cols)

    def remote(src, dst, ssem, rsem, k):
        return pltpu.make_async_remote_copy(
            src_ref=src, dst_ref=dst, send_sem=ssem, recv_sem=rsem,
            device_id={"island": ahead(k)}, device_id_type=MESH)

    def drain(ref, sem):
        pltpu.make_async_copy(ref, ref, sem).wait()

    small = [pltpu.make_async_copy(path_hbm, path, load_sem.at[0]),
             pltpu.make_async_copy(owner_hbm, owner, load_sem.at[1]),
             pltpu.make_async_copy(outer_hbm.at[0, 0], outer_v, load_sem.at[2]),
             pltpu.make_async_copy(mom_hbm.at[0, 0], mom_v, load_sem.at[3])]
    own = [pltpu.make_async_copy(p_hbm.at[0, :, :, span(me, c)], arrived[c].at[peers, 0:2], self_sem.at[c])
           for c in range(chunks)]
    for copy in small + own:
        copy.start()
    barrier = pltpu.get_barrier_semaphore()
    for k in range(peers):
        pl.semaphore_signal(barrier, inc=1, device_id={"island": ahead(k)}, device_id_type=MESH)
    pl.semaphore_wait(barrier, peers)

    def send_params(c):
        for k in range(peers):
            remote(p_hbm.at[0, :, :, span(ahead(k), c)], arrived[c].at[k, 0:2],
                   send_p.at[c], recv_p.at[c], k).start()

    def send_base(c):
        for k in range(peers):
            remote(base_v.at[:, span(ahead(k), c)], arrived[c].at[k, 2],
                   send_b.at[c], recv_b.at[c], k).start()

    send_params(0)
    for copy in small:
        copy.wait()
    mine = owner[0, me]
    used = jnp.int32(0)
    for j in range(n):
        for level in range(2):
            used += (path[level, j] == mine).astype(jnp.int32)
    hit = jnp.minimum(used, 1).astype(jnp.float32)
    base_v[...] = (1.0 - both_rates * hit) * outer_v[...] - (
        outer_rate * momentum_rate * momentum_rate) * mom_v[...]
    send_base(0)
    for c in range(1, chunks):
        send_params(c)
        send_base(c)
    for c in range(chunks):
        arrived[c][peers, 2] = base_v[:, span(me, c)]

    sources = [behind(k) for k in range(peers)] + [me]
    for m in range(n):
        level = m // ring
        count = jnp.int32(0)
        holder = jnp.int32(0)
        for k in range(n):
            count += (path[level, sources[k]] == m).astype(jnp.int32)
            holder = jnp.where(owner[0, sources[k]] == m, jnp.int32(k), holder)
        slot_of[m] = holder
        rate = both_rates / jnp.maximum(jnp.full((1, 128), count.astype(jnp.float32)), 1.0)
        for k in range(n):
            weights[pl.ds(m * n + k, 1), :] = rate * (path[level, sources[k]] == m).astype(jnp.float32)

    for c in range(chunks):
        own[c].wait()
        drain(arrived[c].at[0:peers, 0:2], recv_p.at[c])
        drain(arrived[c].at[0:peers, 2], recv_b.at[c])
        for level in range(2):
            acc = [arrived[c][slot_of[level * ring + m], 2] for m in range(ring)]
            for k in range(n):
                v = arrived[c][k, level]
                for m in range(ring):
                    w = weights[pl.ds((level * ring + m) * n + k, 1), :]
                    if cols > 128:
                        w = jnp.concatenate([w] * (cols // 128), axis=1)
                    acc[m] = acc[m] + w * v
            for m in range(ring):
                table[c, level * ring + m] = acc[m]
        for k in range(n):
            to = ahead(k) if k < peers else me
            stage[c, k, 0] = table[c, path[0, to]]
            stage[c, k, 1] = table[c, path[1, to]]
            stage[c, k, 2] = table[c, owner[0, to]]
            if k < peers:
                remote(stage.at[c, k], home.at[:, :, span(me, c)], send_u.at[c], recv_u.at[c], k).start()
        pltpu.make_async_copy(stage.at[c, peers], home.at[:, :, span(me, c)], self_sem.at[c]).start()
    for c in range(chunks):
        pltpu.make_async_copy(stage.at[c, peers], home.at[:, :, span(me, c)], self_sem.at[c]).wait()
        drain(stage.at[c, 0:peers], recv_u.at[c])
    for c in range(chunks):
        drain(arrived[c].at[0:peers, 0:2], send_p.at[c])
        drain(arrived[c].at[0:peers, 2], send_b.at[c])
        drain(stage.at[c, 0:peers], send_u.at[c])


def finish(home, outer_hbm, mom_hbm, par_out, outer_out, mom_out, home_v, outer_v, mom_v, new_v, load_sem, store_sem):
    loads = [pltpu.make_async_copy(home.at[2], home_v.at[2], load_sem.at[0]),
             pltpu.make_async_copy(outer_hbm.at[0, 0], outer_v, load_sem.at[1]),
             pltpu.make_async_copy(mom_hbm.at[0, 0], mom_v, load_sem.at[2]),
             pltpu.make_async_copy(home.at[0], home_v.at[0], load_sem.at[3]),
             pltpu.make_async_copy(home.at[1], home_v.at[1], load_sem.at[4])]
    stores = [pltpu.make_async_copy(home_v.at[2], outer_out.at[0, 0], store_sem.at[0]),
              pltpu.make_async_copy(home_v.at[0], par_out.at[0, 0], store_sem.at[1]),
              pltpu.make_async_copy(home_v.at[1], par_out.at[0, 1], store_sem.at[2]),
              pltpu.make_async_copy(new_v, mom_out.at[0, 0], store_sem.at[3])]
    for copy in loads:
        copy.start()
    loads[0].wait()
    stores[0].start()
    loads[1].wait()
    loads[2].wait()
    new_v[...] = ((outer_v[...] - home_v[2]) * (1.0 / outer_rate) + momentum_rate * mom_v[...]) * (
        1.0 / (1.0 + momentum_rate))
    stores[3].start()
    loads[3].wait()
    stores[1].start()
    loads[4].wait()
    stores[2].start()
    for copy in stores:
        copy.wait()


def body(island_params, outer_params, momentum, path_modules, owner_modules):
    n = path_modules.shape[0]
    depth, width = island_params.shape[2:]
    cols = width // n // chunks
    f32 = jnp.float32
    hbm = pl.BlockSpec(memory_space=pltpu.HBM)
    dma = pltpu.SemaphoreType.DMA
    home = pl.pallas_call(
        functools.partial(relay, n),
        out_shape=jax.ShapeDtypeStruct((3, depth, width), f32),
        in_specs=[hbm] * 5,
        out_specs=hbm,
        scratch_shapes=[
            pltpu.SMEM((2, n), jnp.int32),
            pltpu.SMEM((1, n), jnp.int32),
            pltpu.VMEM((depth, width), f32),
            pltpu.VMEM((depth, width), f32),
            pltpu.VMEM((depth, width), f32),
            pltpu.VMEM((chunks, n, depth, cols), f32),
            pltpu.VMEM((chunks, n, 3, depth, cols), f32),
            pltpu.VMEM((n * n, 128), f32),
            pltpu.SMEM((n,), jnp.int32),
            dma((4,)),
        ] + [dma((chunks,))] * 7 + [pltpu.VMEM((n, 3, depth, cols), f32)] * chunks,
        compiler_params=pltpu.CompilerParams(collective_id=1, has_side_effects=True, vmem_limit_bytes=ROOM),
        name="outer_step",
    )(island_params, outer_params, momentum, path_modules.T, owner_modules.T)
    return pl.pallas_call(
        finish,
        out_shape=tuple(jax.ShapeDtypeStruct(a.shape, f32) for a in (island_params, outer_params, momentum)),
        in_specs=[hbm] * 3,
        out_specs=(hbm,) * 3,
        scratch_shapes=[
            pltpu.VMEM((3, depth, width), f32),
            pltpu.VMEM((depth, width), f32),
            pltpu.VMEM((depth, width), f32),
            pltpu.VMEM((depth, width), f32),
            dma((5,)),
            dma((4,)),
        ],
        compiler_params=pltpu.CompilerParams(vmem_limit_bytes=ROOM),
        name="finish",
    )(home, outer_params, momentum)


def solution(mesh):
    split = P("island", None, "shard", None)
    return jax.shard_map(
        body,
        mesh=mesh,
        in_specs=(split, split, split, P(), P()),
        out_specs=(split, split, split),
        check_vma=False,
    )
```

time: 334 us -> 33.6 us (0.10)
  waiting for transfers between devices: 300 us -> 0 us
  Pallas kernels: 0 us -> 32.8 us
  between operations: 16.7 us -> 0.64 us
  other arithmetic: 9.41 us -> 0 us
  local copies, waits for them, and re-layouts: 7.36 us -> 0 us
    psum x2 -> x0, waiting for transfers between devices: 300 us -> none  [the longest x1 151 us: body(): summed_all = lax.psum(placed, 'island')]
    pallas_call x0 -> x2, Pallas kernels: none -> 32.8 us  [the longest x1 30.9 us: body(): pl.pallas_call(functools.partial(relay, n), out_shape=jax.ShapeDtypeStruc...]
  transfers between devices with their start and end apart: 2 -> 0, of which waited for: 2 -> 0; matrix products, arithmetic and copies ran while one was open for 1% -> 0% of each run, Pallas kernels for 0% -> 0%
where the time goes in v2:
time: 33.6 us; the launch traced here: 33.4 us
  Pallas kernels  32.8 us (98%)
  between operations  0.64 us (2%)
    pallas_call x1, Pallas kernels, body(): pl.pallas_call(functools.partial(relay, n), out_shape=jax.ShapeDtypeStruc...  30.9 us
    pallas_call x1, Pallas kernels, body(): pl.pallas_call(finish, out_shape=tuple((jax.ShapeDtypeStruct(a.shape, f32...  1.9 us

profile of v2, /device:TPU:56, one launch (start us, length us, event | category | flops | bytes accessed | tf_op | source)
XLA Modules:
  0.0 33.4 jit_solution(15268373607912944198)
XLA Ops:
  0.6 30.9 %outer_step.1.home = f32[3,8,4096]{2,1,0:T(8,128)} custom-call(f32[1,2,8,4096]{3,2,1,0:T(8,128)} %p_hbm.1, f32[1,1,8,4096]{3,2,1,0:T(8,128)} %outer_hbm.3, f32[1,1,8,4096]{3,2,1,0:T(8,128)} %mom_hbm.3, s32[2,16]{1,0:T(2,128)} %bitcast.2, s32[1,16]{1,0:T(1,128)} %bitcast.3), custom_call_target="tpu_custom_call" | custom-call | tf_op jit(solution)/shard_map/outer_step/pallas_call | solution.py:169
  31.5 1.9 %finish.1 = (f32[1,2,8,4096]{3,2,1,0:T(8,128)}, f32[1,1,8,4096]{3,2,1,0:T(8,128)}, f32[1,1,8,4096]{3,2,1,0:T(8,128)}) custom-call(f32[3,8,4096]{2,1,0:T(8,128)} %outer_step.1.home, f32[1,1,8,4096]{3,2,1,0:T(8,128)} %outer_hbm.3, f32[1,1,8,4096]{3,2,1,0:T(8,128)} %mom_hbm.3), custom_call_target="tpu_custom_call" | custom-call | tf_op jit(solution)/shard_map/finish/pallas_call | solution.py:189

commit v3 on v2

--- a/solution.py
+++ b/solution.py
@@ -11,7 +11,7 @@
 outer_rate = 0.7
 both_rates = outer_rate * (1.0 + momentum_rate)
 MESH = pl.DeviceIdType.MESH
-ROOM = 60 * 1024 * 1024
+ROOM = 16 * 1024 * 1024
 chunks = 2
 
 
@@ -121,40 +121,25 @@
             stage[c, k, 1] = table[c, path[1, to]]
             stage[c, k, 2] = table[c, owner[0, to]]
             if k < peers:
-                remote(stage.at[c, k], home.at[:, :, span(me, c)], send_u.at[c], recv_u.at[c], k).start()
-        pltpu.make_async_copy(stage.at[c, peers], home.at[:, :, span(me, c)], self_sem.at[c]).start()
+                remote(stage.at[c, k], home.at[0:3, :, span(me, c)], send_u.at[c], recv_u.at[c], k).start()
+        pltpu.make_async_copy(stage.at[c, peers], home.at[0:3, :, span(me, c)], self_sem.at[c]).start()
     for c in range(chunks):
-        pltpu.make_async_copy(stage.at[c, peers], home.at[:, :, span(me, c)], self_sem.at[c]).wait()
+        pltpu.make_async_copy(stage.at[c, peers], home.at[0:3, :, span(me, c)], self_sem.at[c]).wait()
         drain(stage.at[c, 0:peers], recv_u.at[c])
+    home[3] = ((outer_v[...] - home[2]) * (1.0 / outer_rate) + momentum_rate * mom_v[...]) * (
+        1.0 / (1.0 + momentum_rate))
     for c in range(chunks):
         drain(arrived[c].at[0:peers, 0:2], send_p.at[c])
         drain(arrived[c].at[0:peers, 2], send_b.at[c])
         drain(stage.at[c, 0:peers], send_u.at[c])
 
 
-def finish(home, outer_hbm, mom_hbm, par_out, outer_out, mom_out, home_v, outer_v, mom_v, new_v, load_sem, store_sem):
-    loads = [pltpu.make_async_copy(home.at[2], home_v.at[2], load_sem.at[0]),
-             pltpu.make_async_copy(outer_hbm.at[0, 0], outer_v, load_sem.at[1]),
-             pltpu.make_async_copy(mom_hbm.at[0, 0], mom_v, load_sem.at[2]),
-             pltpu.make_async_copy(home.at[0], home_v.at[0], load_sem.at[3]),
-             pltpu.make_async_copy(home.at[1], home_v.at[1], load_sem.at[4])]
-    stores = [pltpu.make_async_copy(home_v.at[2], outer_out.at[0, 0], store_sem.at[0]),
-              pltpu.make_async_copy(home_v.at[0], par_out.at[0, 0], store_sem.at[1]),
-              pltpu.make_async_copy(home_v.at[1], par_out.at[0, 1], store_sem.at[2]),
-              pltpu.make_async_copy(new_v, mom_out.at[0, 0], store_sem.at[3])]
-    for copy in loads:
+def finish(home, par_out, outer_out, mom_out, sem):
+    stores = [pltpu.make_async_copy(home.at[0:2], par_out.at[0], sem.at[0]),
+              pltpu.make_async_copy(home.at[2], outer_out.at[0, 0], sem.at[1]),
+              pltpu.make_async_copy(home.at[3], mom_out.at[0, 0], sem.at[2])]
+    for copy in stores:
         copy.start()
-    loads[0].wait()
-    stores[0].start()
-    loads[1].wait()
-    loads[2].wait()
-    new_v[...] = ((outer_v[...] - home_v[2]) * (1.0 / outer_rate) + momentum_rate * mom_v[...]) * (
-        1.0 / (1.0 + momentum_rate))
-    stores[3].start()
-    loads[3].wait()
-    stores[1].start()
-    loads[4].wait()
-    stores[2].start()
     for copy in stores:
         copy.wait()
 
@@ -166,11 +151,13 @@
     f32 = jnp.float32
     hbm = pl.BlockSpec(memory_space=pltpu.HBM)
     dma = pltpu.SemaphoreType.DMA
+    ins = [pltpu.with_memory_space_constraint(a, pltpu.HBM) for a in (
+        island_params, outer_params, momentum, path_modules.T, owner_modules.T)]
     home = pl.pallas_call(
         functools.partial(relay, n),
-        out_shape=jax.ShapeDtypeStruct((3, depth, width), f32),
+        out_shape=pltpu.VMEM((4, depth, width), f32),
         in_specs=[hbm] * 5,
-        out_specs=hbm,
+        out_specs=pl.BlockSpec(memory_space=pltpu.VMEM),
         scratch_shapes=[
             pltpu.SMEM((2, n), jnp.int32),
             pltpu.SMEM((1, n), jnp.int32),
@@ -185,23 +172,16 @@
         ] + [dma((chunks,))] * 7 + [pltpu.VMEM((n, 3, depth, cols), f32)] * chunks,
         compiler_params=pltpu.CompilerParams(collective_id=1, has_side_effects=True, vmem_limit_bytes=ROOM),
         name="outer_step",
-    )(island_params, outer_params, momentum, path_modules.T, owner_modules.T)
+    )(*ins)
     return pl.pallas_call(
         finish,
         out_shape=tuple(jax.ShapeDtypeStruct(a.shape, f32) for a in (island_params, outer_params, momentum)),
-        in_specs=[hbm] * 3,
+        in_specs=[pl.BlockSpec(memory_space=pltpu.VMEM)],
         out_specs=(hbm,) * 3,
-        scratch_shapes=[
-            pltpu.VMEM((3, depth, width), f32),
-            pltpu.VMEM((depth, width), f32),
-            pltpu.VMEM((depth, width), f32),
-            pltpu.VMEM((depth, width), f32),
-            dma((5,)),
-            dma((4,)),
-        ],
+        scratch_shapes=[dma((3,))],
         compiler_params=pltpu.CompilerParams(vmem_limit_bytes=ROOM),
         name="finish",
-    )(home, outer_params, momentum)
+    )(home)
 
 
 def solution(mesh):

time: 33.6 us -> 32.4 us (0.964)
  Pallas kernels: 32.8 us -> 31.6 us
    pallas_call x1, Pallas kernels: 1.9 us -> 0.81 us  [body(): pl.pallas_call(finish, out_shape=tuple((jax.ShapeDtypeStruct(a.shape, f32...]
where the time goes in v3:
time: 32.4 us; the launch traced here: 32.3 us
  Pallas kernels  31.6 us (98%)
  between operations  0.64 us (2%)
    pallas_call x1, Pallas kernels, body(): pl.pallas_call(functools.partial(relay, n), out_shape=pltpu.VMEM((4, dept...  30.8 us
    pallas_call x1, Pallas kernels, body(): pl.pallas_call(finish, out_shape=tuple((jax.ShapeDtypeStruct(a.shape, f32...  0.81 us

profile of v3, /device:TPU:56, one launch (start us, length us, event | category | flops | bytes accessed | tf_op | source)
XLA Modules:
  0.0 32.3 jit_solution(3443783425685046831)
XLA Ops:
  0.6 30.8 %outer_step.1.home = f32[4,8,4096]{2,1,0:T(8,128)S(1)} custom-call(f32[1,2,8,4096]{3,2,1,0:T(8,128)} %p_hbm.1, f32[1,1,8,4096]{3,2,1,0:T(8,128)} %outer_hbm.1, f32[1,1,8,4096]{3,2,1,0:T(8,128)} %mom_hbm.1, s32[2,16]{1,0:T(2,128)} %bitcast.2, s32[1,16]{1,0:T(1,128)} %bitcast.3), custom_call_target="tpu_custom_call" | custom-call | tf_op jit(solution)/shard_map/outer_step/pallas_call | solution.py:156
  31.5 0.8 %finish.1 = (f32[1,2,8,4096]{3,2,1,0:T(8,128)}, f32[1,1,8,4096]{3,2,1,0:T(8,128)}, f32[1,1,8,4096]{3,2,1,0:T(8,128)}) custom-call(f32[4,8,4096]{2,1,0:T(8,128)S(1)} %outer_step.1.home), custom_call_target="tpu_custom_call" | custom-call | tf_op jit(solution)/shard_map/finish/pallas_call | solution.py:176

commit v4 on v3

--- a/solution.py
+++ b/solution.py
@@ -16,8 +16,9 @@
 
 
 def relay(n, p_hbm, outer_hbm, mom_hbm, path_hbm, owner_hbm, home,
-          path, owner, outer_v, mom_v, base_v, table, stage, weights, slot_of,
-          load_sem, self_sem, send_p, recv_p, send_b, recv_b, send_u, recv_u, *arrived):
+          path, owner, outer_v, mom_v, mine_v, table, stage, weights, slot_of,
+          load_sem, self_sem, send_p, recv_p, send_u, recv_u, *slots):
+    arrived = slots[:chunks]
     me = lax.axis_index("island")
     ring = n // 2
     width = outer_v.shape[1]
@@ -43,33 +44,24 @@
             src_ref=src, dst_ref=dst, send_sem=ssem, recv_sem=rsem,
             device_id={"island": ahead(k)}, device_id_type=MESH)
 
+    def deliver(c, t):
+        pltpu.make_async_remote_copy(
+            src_ref=stage.at[c, t], dst_ref=home.at[0:3, :, span(me, c)], send_sem=send_u.at[c], recv_sem=recv_u.at[c],
+            device_id={"island": t}, device_id_type=MESH).start()
+
     def drain(ref, sem):
         pltpu.make_async_copy(ref, ref, sem).wait()
 
     small = [pltpu.make_async_copy(path_hbm, path, load_sem.at[0]),
              pltpu.make_async_copy(owner_hbm, owner, load_sem.at[1]),
              pltpu.make_async_copy(outer_hbm.at[0, 0], outer_v, load_sem.at[2]),
-             pltpu.make_async_copy(mom_hbm.at[0, 0], mom_v, load_sem.at[3])]
-    own = [pltpu.make_async_copy(p_hbm.at[0, :, :, span(me, c)], arrived[c].at[peers, 0:2], self_sem.at[c])
-           for c in range(chunks)]
-    for copy in small + own:
+             pltpu.make_async_copy(mom_hbm.at[0, 0], mom_v, load_sem.at[3]),
+             pltpu.make_async_copy(p_hbm.at[0], mine_v.at[0:2], load_sem.at[4])]
+    for copy in small:
         copy.start()
     barrier = pltpu.get_barrier_semaphore()
     for k in range(peers):
         pl.semaphore_signal(barrier, inc=1, device_id={"island": ahead(k)}, device_id_type=MESH)
-    pl.semaphore_wait(barrier, peers)
-
-    def send_params(c):
-        for k in range(peers):
-            remote(p_hbm.at[0, :, :, span(ahead(k), c)], arrived[c].at[k, 0:2],
-                   send_p.at[c], recv_p.at[c], k).start()
-
-    def send_base(c):
-        for k in range(peers):
-            remote(base_v.at[:, span(ahead(k), c)], arrived[c].at[k, 2],
-                   send_b.at[c], recv_b.at[c], k).start()
-
-    send_params(0)
     for copy in small:
         copy.wait()
     mine = owner[0, me]
@@ -78,14 +70,13 @@
         for level in range(2):
             used += (path[level, j] == mine).astype(jnp.int32)
     hit = jnp.minimum(used, 1).astype(jnp.float32)
-    base_v[...] = (1.0 - both_rates * hit) * outer_v[...] - (
+    mine_v[2] = (1.0 - both_rates * hit) * outer_v[...] - (
         outer_rate * momentum_rate * momentum_rate) * mom_v[...]
-    send_base(0)
-    for c in range(1, chunks):
-        send_params(c)
-        send_base(c)
+    pl.semaphore_wait(barrier, peers)
     for c in range(chunks):
-        arrived[c][peers, 2] = base_v[:, span(me, c)]
+        for k in range(peers):
+            remote(mine_v.at[:, :, span(ahead(k), c)], arrived[c].at[k], send_p.at[c], recv_p.at[c], k).start()
+        arrived[c][peers] = mine_v[:, :, span(me, c)]
 
     sources = [behind(k) for k in range(peers)] + [me]
     for m in range(n):
@@ -101,9 +92,7 @@
             weights[pl.ds(m * n + k, 1), :] = rate * (path[level, sources[k]] == m).astype(jnp.float32)
 
     for c in range(chunks):
-        own[c].wait()
-        drain(arrived[c].at[0:peers, 0:2], recv_p.at[c])
-        drain(arrived[c].at[0:peers, 2], recv_b.at[c])
+        drain(arrived[c].at[0:peers], recv_p.at[c])
         for level in range(2):
             acc = [arrived[c][slot_of[level * ring + m], 2] for m in range(ring)]
             for k in range(n):
@@ -115,22 +104,22 @@
                     acc[m] = acc[m] + w * v
             for m in range(ring):
                 table[c, level * ring + m] = acc[m]
-        for k in range(n):
-            to = ahead(k) if k < peers else me
-            stage[c, k, 0] = table[c, path[0, to]]
-            stage[c, k, 1] = table[c, path[1, to]]
-            stage[c, k, 2] = table[c, owner[0, to]]
-            if k < peers:
-                remote(stage.at[c, k], home.at[0:3, :, span(me, c)], send_u.at[c], recv_u.at[c], k).start()
-        pltpu.make_async_copy(stage.at[c, peers], home.at[0:3, :, span(me, c)], self_sem.at[c]).start()
+        for t in [0, 1, 2, 3, 4, 5, 6, 7, 8, 9, 10, 11, 12, 13, 14, 15]:
+            stage[c, t, 0] = table[c, path[0, t]]
+            stage[c, t, 1] = table[c, path[1, t]]
+            stage[c, t, 2] = table[c, owner[0, t]]
+
+            @pl.when(t != me)
+            def _():
+                deliver(c, t)
+        home[0:3, :, span(me, c)] = stage[c, me]
+
     for c in range(chunks):
-        pltpu.make_async_copy(stage.at[c, peers], home.at[0:3, :, span(me, c)], self_sem.at[c]).wait()
         drain(stage.at[c, 0:peers], recv_u.at[c])
     home[3] = ((outer_v[...] - home[2]) * (1.0 / outer_rate) + momentum_rate * mom_v[...]) * (
         1.0 / (1.0 + momentum_rate))
     for c in range(chunks):
-        drain(arrived[c].at[0:peers, 0:2], send_p.at[c])
-        drain(arrived[c].at[0:peers, 2], send_b.at[c])
+        drain(arrived[c].at[0:peers], send_p.at[c])
         drain(stage.at[c, 0:peers], send_u.at[c])
 
 
@@ -163,13 +152,13 @@
             pltpu.SMEM((1, n), jnp.int32),
             pltpu.VMEM((depth, width), f32),
             pltpu.VMEM((depth, width), f32),
-            pltpu.VMEM((depth, width), f32),
+            pltpu.VMEM((3, depth, width), f32),
             pltpu.VMEM((chunks, n, depth, cols), f32),
             pltpu.VMEM((chunks, n, 3, depth, cols), f32),
             pltpu.VMEM((n * n, 128), f32),
             pltpu.SMEM((n,), jnp.int32),
-            dma((4,)),
-        ] + [dma((chunks,))] * 7 + [pltpu.VMEM((n, 3, depth, cols), f32)] * chunks,
+            dma((5,)),
+        ] + [dma((chunks,))] * 5 + [pltpu.VMEM((n, 3, depth, cols), f32)] * chunks,
         compiler_params=pltpu.CompilerParams(collective_id=1, has_side_effects=True, vmem_limit_bytes=ROOM),
         name="outer_step",
     )(*ins)

time: 32.4 us -> 31.2 us (0.963)
  Pallas kernels: 31.6 us -> 30.1 us
    pallas_call x1, Pallas kernels: 30.8 us -> 29.3 us  [body(): pl.pallas_call(functools.partial(relay, n), out_shape=pltpu.VMEM((4, dept...]
where the time goes in v4:
time: 31.2 us; the launch traced here: 30.8 us
  Pallas kernels  30.1 us (96%)
  between operations  0.64 us (2%)
    pallas_call x1, Pallas kernels, body(): pl.pallas_call(functools.partial(relay, n), out_shape=pltpu.VMEM((4, dept...  29.3 us
    pallas_call x1, Pallas kernels, body(): pl.pallas_call(finish, out_shape=tuple((jax.ShapeDtypeStruct(a.shape, f32...  0.81 us

profile of v4, /device:TPU:56, one launch (start us, length us, event | category | flops | bytes accessed | tf_op | source)
XLA Modules:
  0.0 30.8 jit_solution(9466535806486074801)
XLA Ops:
  0.6 29.3 %outer_step.1.home = f32[4,8,4096]{2,1,0:T(8,128)S(1)} custom-call(f32[1,2,8,4096]{3,2,1,0:T(8,128)} %p_hbm.1, f32[1,1,8,4096]{3,2,1,0:T(8,128)} %outer_hbm.1, f32[1,1,8,4096]{3,2,1,0:T(8,128)} %mom_hbm.1, s32[2,16]{1,0:T(2,128)} %bitcast.2, s32[1,16]{1,0:T(1,128)} %bitcast.3), custom_call_target="tpu_custom_call" | custom-call | tf_op jit(solution)/shard_map/outer_step/pallas_call | solution.py:145
  30.0 0.8 %finish.1 = (f32[1,2,8,4096]{3,2,1,0:T(8,128)}, f32[1,1,8,4096]{3,2,1,0:T(8,128)}, f32[1,1,8,4096]{3,2,1,0:T(8,128)}) custom-call(f32[4,8,4096]{2,1,0:T(8,128)S(1)} %outer_step.1.home), custom_call_target="tpu_custom_call" | custom-call | tf_op jit(solution)/shard_map/finish/pallas_call | solution.py:165

commit v5 on v4

--- a/solution.py
+++ b/solution.py
@@ -20,6 +20,7 @@
           load_sem, self_sem, send_p, recv_p, send_u, recv_u, *slots):
     arrived = slots[:chunks]
     me = lax.axis_index("island")
+    core = lax.axis_index("shard") % 2
     ring = n // 2
     width = outer_v.shape[1]
     cols = width // n // chunks
@@ -74,6 +75,11 @@
         outer_rate * momentum_rate * momentum_rate) * mom_v[...]
     pl.semaphore_wait(barrier, peers)
     for c in range(chunks):
+        if c == 1:
+            @pl.when(core == 1)
+            def _():
+                drain(arrived[0].at[0:peers], send_p.at[0])
+
         for k in range(peers):
             remote(mine_v.at[:, :, span(ahead(k), c)], arrived[c].at[k], send_p.at[c], recv_p.at[c], k).start()
         arrived[c][peers] = mine_v[:, :, span(me, c)]
@@ -119,7 +125,12 @@
     home[3] = ((outer_v[...] - home[2]) * (1.0 / outer_rate) + momentum_rate * mom_v[...]) * (
         1.0 / (1.0 + momentum_rate))
     for c in range(chunks):
-        drain(arrived[c].at[0:peers], send_p.at[c])
+        if c == 0:
+            @pl.when(core == 0)
+            def _():
+                drain(arrived[c].at[0:peers], send_p.at[c])
+        else:
+            drain(arrived[c].at[0:peers], send_p.at[c])
         drain(stage.at[c, 0:peers], send_u.at[c])
 
 

time: 31.2 us -> 30.4 us (0.974)
  the two profiles are of different devices: /device:TPU:56 before, /device:TPU:1 now
where the time goes in v5:
time: 30.4 us; the launch traced here: 30.3 us
  Pallas kernels  29.6 us (97%)
  between operations  0.64 us (2%)
    pallas_call x1, Pallas kernels, body(): pl.pallas_call(functools.partial(relay, n), out_shape=pltpu.VMEM((4, dept...  28.8 us
    pallas_call x1, Pallas kernels, body(): pl.pallas_call(finish, out_shape=tuple((jax.ShapeDtypeStruct(a.shape, f32...  0.81 us

profile of v5, /device:TPU:1, one launch (start us, length us, event | category | flops | bytes accessed | tf_op | source)
XLA Modules:
  0.0 30.3 jit_solution(14323324747858096864)
XLA Ops:
  0.6 28.8 %outer_step.1.home = f32[4,8,4096]{2,1,0:T(8,128)S(1)} custom-call(f32[1,2,8,4096]{3,2,1,0:T(8,128)} %p_hbm.1, f32[1,1,8,4096]{3,2,1,0:T(8,128)} %outer_hbm.1, f32[1,1,8,4096]{3,2,1,0:T(8,128)} %mom_hbm.1, s32[2,16]{1,0:T(2,128)} %bitcast.2, s32[1,16]{1,0:T(1,128)} %bitcast.3), custom_call_target="tpu_custom_call" | custom-call | tf_op jit(solution)/shard_map/outer_step/pallas_call | solution.py:156
  29.5 0.8 %finish.1 = (f32[1,2,8,4096]{3,2,1,0:T(8,128)}, f32[1,1,8,4096]{3,2,1,0:T(8,128)}, f32[1,1,8,4096]{3,2,1,0:T(8,128)}) custom-call(f32[4,8,4096]{2,1,0:T(8,128)S(1)} %outer_step.1.home), custom_call_target="tpu_custom_call" | custom-call | tf_op jit(solution)/shard_map/finish/pallas_call | solution.py:176

commit v6 on v5

--- a/solution.py
+++ b/solution.py
@@ -31,11 +31,13 @@
 
     def ahead(k):
         dz, dx = offsets[k]
-        return lax.rem(z + dz, ring) * 2 + lax.rem(x + dx, 2)
+        turn = jnp.where(core == 1, ring - dz, dz)
+        return lax.rem(z + turn, ring) * 2 + lax.rem(x + dx, 2)
 
     def behind(k):
         dz, dx = offsets[k]
-        return lax.rem(z + ring - dz, ring) * 2 + lax.rem(x + dx, 2)
+        turn = jnp.where(core == 1, dz, ring - dz)
+        return lax.rem(z + turn, ring) * 2 + lax.rem(x + dx, 2)
 
     def span(j, c):
         return pl.ds(pl.multiple_of(j * (cols * chunks) + c * cols, cols), cols)
@@ -122,8 +124,10 @@
 
     for c in range(chunks):
         drain(stage.at[c, 0:peers], recv_u.at[c])
-    home[3] = ((outer_v[...] - home[2]) * (1.0 / outer_rate) + momentum_rate * mom_v[...]) * (
-        1.0 / (1.0 + momentum_rate))
+        for j in range(n):
+            there = span(j, c)
+            home[3, :, there] = ((outer_v[:, there] - home[2, :, there]) * (1.0 / outer_rate)
+                                 + momentum_rate * mom_v[:, there]) * (1.0 / (1.0 + momentum_rate))
     for c in range(chunks):
         if c == 0:
             @pl.when(core == 0)

time: 30.4 us -> 30.4 us (level)
  no operation moved by 1% of the time
where the time goes in v6:
time: 30.4 us; the launch traced here: 30.3 us
  Pallas kernels  29.6 us (97%)
  between operations  0.64 us (2%)
    pallas_call x1, Pallas kernels, body(): pl.pallas_call(functools.partial(relay, n), out_shape=pltpu.VMEM((4, dept...  28.8 us
    pallas_call x1, Pallas kernels, body(): pl.pallas_call(finish, out_shape=tuple((jax.ShapeDtypeStruct(a.shape, f32...  0.81 us

profile of v6, /device:TPU:1, one launch (start us, length us, event | category | flops | bytes accessed | tf_op | source)
XLA Modules:
  0.0 30.3 jit_solution(6561967477269751537)
XLA Ops:
  0.6 28.8 %outer_step.1.home = f32[4,8,4096]{2,1,0:T(8,128)S(1)} custom-call(f32[1,2,8,4096]{3,2,1,0:T(8,128)} %p_hbm.1, f32[1,1,8,4096]{3,2,1,0:T(8,128)} %outer_hbm.1, f32[1,1,8,4096]{3,2,1,0:T(8,128)} %mom_hbm.1, s32[2,16]{1,0:T(2,128)} %bitcast.2, s32[1,16]{1,0:T(1,128)} %bitcast.3), custom_call_target="tpu_custom_call" | custom-call | tf_op jit(solution)/shard_map/outer_step/pallas_call | solution.py:160
  29.5 0.8 %finish.1 = (f32[1,2,8,4096]{3,2,1,0:T(8,128)}, f32[1,1,8,4096]{3,2,1,0:T(8,128)}, f32[1,1,8,4096]{3,2,1,0:T(8,128)}) custom-call(f32[4,8,4096]{2,1,0:T(8,128)S(1)} %outer_step.1.home), custom_call_target="tpu_custom_call" | custom-call | tf_op jit(solution)/shard_map/finish/pallas_call | solution.py:180

commit v7 on v6

--- a/solution.py
+++ b/solution.py
@@ -47,10 +47,10 @@
             src_ref=src, dst_ref=dst, send_sem=ssem, recv_sem=rsem,
             device_id={"island": ahead(k)}, device_id_type=MESH)
 
-    def deliver(c, t):
+    def deliver(c, i, to):
         pltpu.make_async_remote_copy(
-            src_ref=stage.at[c, t], dst_ref=home.at[0:3, :, span(me, c)], send_sem=send_u.at[c], recv_sem=recv_u.at[c],
-            device_id={"island": t}, device_id_type=MESH).start()
+            src_ref=stage.at[c, i], dst_ref=home.at[0:3, :, span(me, c)], send_sem=send_u.at[c], recv_sem=recv_u.at[c],
+            device_id={"island": to}, device_id_type=MESH).start()
 
     def drain(ref, sem):
         pltpu.make_async_copy(ref, ref, sem).wait()
@@ -112,22 +112,26 @@
                     acc[m] = acc[m] + w * v
             for m in range(ring):
                 table[c, level * ring + m] = acc[m]
-        for t in [0, 1, 2, 3, 4, 5, 6, 7, 8, 9, 10, 11, 12, 13, 14, 15]:
-            stage[c, t, 0] = table[c, path[0, t]]
-            stage[c, t, 1] = table[c, path[1, t]]
-            stage[c, t, 2] = table[c, owner[0, t]]
-
-            @pl.when(t != me)
+        orders = (([0, 1, 2, 3, 4, 5, 6, 7, 8, 9, 10, 11, 12, 13, 14, 15], [0, 1, 2, 3, 4, 5, 6, 7, 8, 9, 10, 11, 12, 13, 14, 15]),
+                  ([0, 1, 2, 3, 8, 9, 10, 11, 12, 13, 14, 15, 4, 5, 6, 7], [0, 1, 2, 3, 4, 5, 6, 7, 8, 9, 10, 11, 12, 13, 14, 15]))
+        for i, (early, late) in enumerate(zip(*orders[c])):
+            to = jnp.where(me < n // 2, early, late)
+            stage[c, i, 0] = table[c, path[0, to]]
+            stage[c, i, 1] = table[c, path[1, to]]
+            stage[c, i, 2] = table[c, owner[0, to]]
+
+            @pl.when(to != me)
             def _():
-                deliver(c, t)
-        home[0:3, :, span(me, c)] = stage[c, me]
+                deliver(c, i, to)
+
+        home[0, :, span(me, c)] = table[c, path[0, me]]
+        home[1, :, span(me, c)] = table[c, path[1, me]]
+        home[2, :, span(me, c)] = table[c, owner[0, me]]
 
     for c in range(chunks):
         drain(stage.at[c, 0:peers], recv_u.at[c])
-        for j in range(n):
-            there = span(j, c)
-            home[3, :, there] = ((outer_v[:, there] - home[2, :, there]) * (1.0 / outer_rate)
-                                 + momentum_rate * mom_v[:, there]) * (1.0 / (1.0 + momentum_rate))
+    home[3] = ((outer_v[...] - home[2]) * (1.0 / outer_rate) + momentum_rate * mom_v[...]) * (
+        1.0 / (1.0 + momentum_rate))
     for c in range(chunks):
         if c == 0:
             @pl.when(core == 0)

time: 30.4 us -> 30.4 us (level)
  no operation moved by 1% of the time
where the time goes in v7:
time: 30.4 us; the launch traced here: 30.3 us
  Pallas kernels  29.6 us (97%)
  between operations  0.64 us (2%)
    pallas_call x1, Pallas kernels, body(): pl.pallas_call(functools.partial(relay, n), out_shape=pltpu.VMEM((4, dept...  28.8 us
    pallas_call x1, Pallas kernels, body(): pl.pallas_call(finish, out_shape=tuple((jax.ShapeDtypeStruct(a.shape, f32...  0.81 us

profile of v7, /device:TPU:1, one launch (start us, length us, event | category | flops | bytes accessed | tf_op | source)
XLA Modules:
  0.0 30.3 jit_solution(14833272138713957522)
XLA Ops:
  0.6 28.8 %outer_step.1.home = f32[4,8,4096]{2,1,0:T(8,128)S(1)} custom-call(f32[1,2,8,4096]{3,2,1,0:T(8,128)} %p_hbm.1, f32[1,1,8,4096]{3,2,1,0:T(8,128)} %outer_hbm.1, f32[1,1,8,4096]{3,2,1,0:T(8,128)} %mom_hbm.1, s32[2,16]{1,0:T(2,128)} %bitcast.2, s32[1,16]{1,0:T(1,128)} %bitcast.3), custom_call_target="tpu_custom_call" | custom-call | tf_op jit(solution)/shard_map/outer_step/pallas_call | solution.py:164
  29.5 0.8 %finish.1 = (f32[1,2,8,4096]{3,2,1,0:T(8,128)}, f32[1,1,8,4096]{3,2,1,0:T(8,128)}, f32[1,1,8,4096]{3,2,1,0:T(8,128)}) custom-call(f32[4,8,4096]{2,1,0:T(8,128)S(1)} %outer_step.1.home), custom_call_target="tpu_custom_call" | custom-call | tf_op jit(solution)/shard_map/finish/pallas_call | solution.py:184
